TPU v7x, 32 devices: a whole 2x2x4 slice. The times are simulated.
32 devices in a mesh: leaf: 8 (over z, core), vec: 4 (over y, x).
Axes of the slice: x: 2, y: 2, z: 4, core: 2. Of those that a mesh axis runs over, the one named last changes fastest.
Arguments:
- points: bfloat16 [128, 3, 256], P('leaf'), may hold values from 0 to 1
- probe_vectors: bfloat16 [128, 256, 256], P('leaf', 'vec'), may hold values from -6 to 6
- neighbours: int32 [128, 16], P('leaf'), may hold values from -1 to 127, as said below
- leaf_pivots: int32 [128, 64], P('leaf'), may hold values from 0 to 255, as said below
- leaf_inverse: float32 [128, 64, 64], P('leaf'), as said below
- local_pivots: int32 [120, 64], P('leaf'), may hold values from 0 to 127, as said below
- local_inverse: float32 [120, 64, 64], P('leaf'), as said below
- upper_pivots: int32 [7, 64], replicated, may hold values from 0 to 127, as said below
- upper_inverse: float32 [7, 64, 64], replicated, as said below
Outputs:
- leaf_interp: float32 [128, 256, 64], P('leaf')
- local_interp: float32 [120, 128, 64], P('leaf')
- upper_interp: float32 [8, 3, 128, 64], P('leaf')
- top_sketch: float32 [8, 256, 64], P('leaf', 'vec')
Inputs may be any that keep to these rules, and one draw needn't show every extreme that they name: Entry 0 of neighbours[i] is i; then come distinct clusters j != i with |j - i| <= 16, then -1 to the end. The first cluster of each group of 16 lists the cluster before it in entry 1, and the last one lists the cluster after it there, where those exist. A list holds at least 4 clusters, and some lists hold 16. `leaf_pivots`: each row holds 64 distinct row numbers. `local_pivots`: each row holds 64 distinct row numbers. `upper_pivots`: each row holds 64 distinct row numbers. `leaf_inverse`: diagonal entries lie in 0.5 to 1.5. `local_inverse`: diagonal entries lie in 0.5 to 1.5. `upper_inverse`: diagonal entries lie in 0.5 to 1.5.
All inputs are finite; a program needn't handle non-finite values.
Results may differ from a plain program's by a relative error of at most 0.0013.
Values may be sent and summed in bfloat16 or wider, within the bound.
No kernel may reach another device: no remote copies, remote signals or barrier semaphores. Data moves between devices by JAX's collectives and lax.ppermute only.
A program may use at most 64 MiB of HBM per device.

v0:
```python
import jax
import jax.numpy as jnp
from jax import lax
from jax.sharding import PartitionSpec as P

UPL = 3


SOFTEN = 0.0009
EPSILON = 1e-06


def padded(shard, sides, width):
    for axis, dim in sides:
        count, length = (lax.axis_size(axis), shard.shape[dim])
        up = [(i, (i + 1) % count) for i in range(count - 1)]
        down = [(j, i) for i, j in up]
        last = lax.slice_in_dim(shard, length - width, length, axis=dim)
        initial = lax.slice_in_dim(shard, 0, width, axis=dim)
        before = lax.ppermute(last, axis, up)
        after = lax.ppermute(initial, axis, down)
        shard = jnp.concatenate([before, shard, after], axis=dim)
    return shard


def shifted(shard, axis, by):
    count = lax.axis_size(axis)
    pairs = [(i, i + by) for i in range(count) if 0 <= i + by < count]
    return lax.ppermute(shard, axis, pairs)


def kernel_tile(near_points, far_points):
    near_xyz = near_points.astype(jnp.float32)
    far_xyz = far_points.astype(jnp.float32)
    distance = SOFTEN + jnp.zeros(
        (near_xyz.shape[0], near_xyz.shape[2], far_xyz.shape[2]), jnp.float32
    )
    for coordinate in range(3):
        offset_gap = near_xyz[:, coordinate, :, None] - far_xyz[:, coordinate, None, :]
        distance = distance + offset_gap * offset_gap
    return 1.0 / (64.0 * jnp.sqrt(distance))


def interpolate(sketch, pivots, inverse, column_total, combine_stats):
    rows = sketch.shape[2]
    index_grid = jnp.broadcast_to(
        pivots[:, None, :], (sketch.shape[0], sketch.shape[1], pivots.shape[1])
    )
    chosen = jnp.take_along_axis(sketch, index_grid, axis=2)
    gram_rows = jnp.einsum("nsp,nsk->npk", sketch, chosen, precision=lax.Precision.HIGHEST)
    squares = jnp.sum(sketch * sketch, axis=(1, 2))
    gram_rows, squares = combine_stats(gram_rows, squares)
    mean_sq = squares / (rows * column_total) + EPSILON
    interp_map = jnp.einsum("npl,nlk->npk", gram_rows, inverse, precision=lax.Precision.HIGHEST)
    interp_map = interp_map / (column_total * mean_sq)[:, None, None]
    upward = jnp.einsum("nsp,npk->nsk", sketch, interp_map, precision=lax.Precision.HIGHEST)
    upward = upward / jnp.sqrt(mean_sq)[:, None, None]
    return (interp_map, upward)


def pair_children(upward):
    node_count = upward.shape[0] // 2
    paired = upward.reshape(node_count, 2, upward.shape[1], upward.shape[2])
    paired = jnp.transpose(paired, (0, 2, 1, 3))
    return paired.reshape(node_count, upward.shape[1], 2 * upward.shape[2])


def on_device(
    points,
    probe_vectors,
    neighbours,
    leaf_pivots,
    leaf_inverse,
    local_pivots,
    local_inverse,
    upper_pivots,
    upper_inverse,
):
    leaf_count = points.shape[0]
    slot_total = neighbours.shape[1]
    columns_here = probe_vectors.shape[1]
    rank_kept = leaf_pivots.shape[1]
    device_index = lax.axis_index("leaf")
    group_total = lax.axis_size("leaf")
    joined = jnp.concatenate([points, probe_vectors], axis=1)
    extended = padded(joined, (("leaf", 0),), leaf_count)
    first_cluster = device_index * leaf_count - leaf_count

    def add_slot(slot_index, running):
        listed = lax.dynamic_slice_in_dim(neighbours, slot_index, 1, 1)[:, 0]
        present = listed >= 0
        position = jnp.clip(listed - first_cluster, 0, 3 * leaf_count - 1)
        blocks = jnp.take(extended, position, axis=0)
        kernel_block = jnp.where(
            present[:, None, None], kernel_tile(points, blocks[:, :3]), 0.0
        ).astype(jnp.bfloat16)
        return running + jnp.einsum(
            "nsq,npq->nsp", blocks[:, 3:], kernel_block, preferred_element_type=jnp.float32
        )

    sketch = lax.fori_loop(
        0, slot_total, add_slot, jnp.zeros((leaf_count, columns_here, points.shape[2]), jnp.float32)
    )
    column_total = columns_here * lax.axis_size("vec")

    def combine_stats(gram_rows, squares):
        return lax.psum((gram_rows, squares), "vec")

    leaf_interp, upward = interpolate(
        sketch, leaf_pivots, leaf_inverse, column_total, combine_stats
    )
    pieces = []
    offset = 0
    while upward.shape[0] > 1:
        node_count = upward.shape[0] // 2
        interp_map, upward = interpolate(
            pair_children(upward),
            local_pivots[offset : offset + node_count],
            local_inverse[offset : offset + node_count],
            column_total,
            combine_stats,
        )
        pieces.append(interp_map)
        offset = offset + node_count
    local_interp = jnp.concatenate(pieces, axis=0)
    own_sketch = upward[0]
    heap_offset = 0
    upper_maps = []
    for tier_index in range(UPL):
        partner = shifted(own_sketch, "leaf", -(1 << tier_index))
        node_index = heap_offset + (device_index >> tier_index + 1)
        interp_map, upward = interpolate(
            jnp.concatenate([own_sketch, partner], axis=1)[None],
            lax.dynamic_slice_in_dim(upper_pivots, node_index, 1, 0),
            lax.dynamic_slice_in_dim(upper_inverse, node_index, 1, 0),
            column_total,
            combine_stats,
        )
        upper_maps.append(interp_map[0])
        own_sketch = upward[0]
        heap_offset = heap_offset + (group_total >> tier_index + 1)
    map_rows = UPL * 2 * rank_kept
    packed = jnp.concatenate(
        [jnp.stack(upper_maps, axis=0).reshape(map_rows, rank_kept), own_sketch], axis=0
    )
    row_number = jnp.arange(packed.shape[0], dtype=jnp.int32)
    row_tier = jnp.minimum(row_number // (2 * rank_kept), UPL)
    for tier_index in reversed(range(UPL)):
        arrived = shifted(packed, "leaf", 1 << tier_index)
        take_rows = (device_index >> tier_index & 1 == 1) & (row_tier >= tier_index)
        packed = jnp.where(take_rows[:, None], arrived, packed)
    stacked = packed[:map_rows].reshape(UPL, 2 * rank_kept, rank_kept)
    own_sketch = packed[map_rows:]
    return (leaf_interp, local_interp, stacked[None], own_sketch[None])


def solution(mesh):
    placed = (
        P("leaf", None, None),
        P("leaf", "vec", None),
        P("leaf", None),
        P("leaf", None),
        P("leaf", None, None),
        P("leaf", None),
        P("leaf", None, None),
        P(),
        P(),
    )
    return jax.shard_map(
        on_device,
        mesh=mesh,
        in_specs=placed,
        out_specs=(
            P("leaf", None, None),
            P("leaf", None, None),
            P("leaf", None, None, None),
            P("leaf", "vec", None),
        ),
        check_vma=False,
    )
```

profile of v0, /device:TPU:0, one launch (start us, length us, event | category | flops | bytes accessed | tf_op | source)
XLA Modules:
  0.0 1659.3 jit_solution(12102567102046889795)
XLA Ops:
  9.4 3.2 collective-permute-start
  30.3 1.8 copy.54
  32.1 107.8 %while.14 = (s32[]{:T(128)}, f32[16,64,256]{2,1,0:T(8,128)S(1)}, s32[16,16]{0,1:T(8,128)S(1)}, s32[]{:T(128)}, bf16[48,67,256]{2,1,0:T(8,128)(2,1)}, /*index=5*/bf16[16,3,256]{2,0,1:T(8,128)(2,1)S(1)}, s32[]{:T(128)}, s32[]{:T(128)}) while((s32[]{:T(128)}, f32[16,64,256]{2,1,0:T(8,128)S(1)}, s32[16,16]{0,1:T(8,128)S(1)}, ...), condition=%wide.region_1.2_spmd.clone, body=%wide.region_0.1_spmd.clone.sunk | while | flops 148673680 | bytes 5362583 | solution.py:101
  32.1 2.1 gather_fusion
  34.4 4.4 fusion.214
  38.9 2.1 gather_fusion
  41.2 4.4 fusion.214
  45.6 2.1 gather_fusion
  47.9 4.4 fusion.214
  52.3 2.1 gather_fusion
  54.6 4.4 fusion.214
  59.1 2.1 gather_fusion
  61.4 4.4 fusion.214
  65.8 2.1 gather_fusion
  68.1 4.4 fusion.214
  72.5 2.1 gather_fusion
  74.9 4.4 fusion.214
  79.3 2.1 gather_fusion
  81.6 4.4 fusion.214
  86.0 2.1 gather_fusion
  88.3 4.4 fusion.214
  92.8 2.1 gather_fusion
  95.1 4.4 fusion.214
  99.5 2.1 gather_fusion
  101.8 4.4 fusion.214
  106.2 2.1 gather_fusion
  108.5 4.4 fusion.214
  113.0 2.1 gather_fusion
  115.3 4.4 fusion.214
  119.7 2.1 gather_fusion
  122.0 4.4 fusion.214
  126.4 2.1 gather_fusion
  128.7 4.4 fusion.214
  133.2 2.1 gather_fusion
  135.5 4.4 fusion.214
  139.9 644.6 %gather_fusion.1 = f32[65536]{0:T(1024)S(1)} fusion(f32[16,64,256]{2,1,0:T(8,128)S(1)} %get-tuple-element.114, s32[65536]{0:T(1024)S(1)} %reshape.429), kind=kCustom, calls=%fused_computation.5 | custom fusion | bytes 1310720 | tf_op jit(solution)/shard_map/jit(take_along_axis)/gather | solution.py:49
  784.7 2.1 fusion.19
  787.9 10.7 psum.113
  798.6 44.8 %all-reduce.9.cloned.1.call-done = f32[16,256,64]{1,2,0:T(8,128)} async-done(((f32[16,256,64]{1,2,0:T(8,128)}), f32[16,256,64]{1,2,0:T(8,128)}) %all-reduce.9.cloned.1.call-update) | async-done | bytes 1048592 | tf_op jit(solution)/shard_map/psum | solution.py:107
  843.4 2.3 convolution_divide_fusion
  847.6 261.8 %gather_fusion.2 = f32[32768]{0:T(1024)S(1)} fusion(f32[8,64,128]{2,1,0:T(8,128)S(1)} %reshape.361, s32[32768]{0:T(1024)S(1)} %copy-done.1), kind=kCustom, calls=%fused_computation.6 | custom fusion | bytes 655360 | tf_op jit(solution)/shard_map/jit(take_along_axis)/gather | solution.py:49
  1111.2 9.1 psum.115
  1120.3 33.7 %all-reduce.11.cloned.1.call-done = f32[8,128,64]{1,2,0:T(8,128)} async-done(((f32[8,128,64]{1,2,0:T(8,128)}), f32[8,128,64]{1,2,0:T(8,128)}) %all-reduce.11.cloned.1.call-update) | async-done | bytes 262160 | tf_op jit(solution)/shard_map/psum | solution.py:107
  1156.7 131.2 %gather_fusion.3 = f32[16384]{0:T(1024)S(1)} fusion(f32[4,64,128]{2,1,0:T(8,128)S(1)} %reshape.363, s32[16384]{0:T(1024)S(1)} %copy-done.2), kind=kCustom, calls=%fused_computation.7 | custom fusion | bytes 327680 | tf_op jit(solution)/shard_map/jit(take_along_axis)/gather | solution.py:49
  1289.1 8.9 psum.117
  1298.0 33.2 %all-reduce.13.cloned.1.call-done = f32[4,128,64]{1,2,0:T(8,128)} async-done(((f32[4,128,64]{1,2,0:T(8,128)}), f32[4,128,64]{1,2,0:T(8,128)}) %all-reduce.13.cloned.1.call-update) | async-done | bytes 131088 | tf_op jit(solution)/shard_map/psum | solution.py:107
  1333.2 65.8 %gather_fusion.4 = f32[8192]{0:T(1024)S(1)} fusion(f32[2,64,128]{2,1,0:T(8,128)S(1)} %reshape.365, s32[8192]{0:T(1024)S(1)} %reshape.447), kind=kCustom, calls=%fused_computation.8 | custom fusion | bytes 163840 | tf_op jit(solution)/shard_map/jit(take_along_axis)/gather | solution.py:49
  1400.0 8.9 psum.119
  1409.0 32.7 %all-reduce.15.cloned.1.call-done = f32[2,128,64]{1,2,0:T(8,128)} async-done(((f32[2,128,64]{1,2,0:T(8,128)}), f32[2,128,64]{1,2,0:T(8,128)}) %all-reduce.15.cloned.1.call-update) | async-done | bytes 65552 | tf_op jit(solution)/shard_map/psum | solution.py:107
  1443.8 25.6 %gather_fusion.5 = f32[4096]{0:T(1024)S(1)} fusion(f32[64,128]{1,0:T(8,128)S(1)} %reshape.367, s32[4096]{0:T(1024)S(1)} %reshape.482), kind=kCustom, calls=%fused_computation.1.clone | custom fusion | bytes 65536 | tf_op jit(solution)/shard_map/jit(take_along_axis)/gather | solution.py:49
  1469.8 16.7 %all-reduce.3 = (f32[128,64]{0,1:T(8,128)S(1)}, f32[1]{0:T(128)}) all-reduce(f32[128,64]{0,1:T(8,128)S(1)} %fusion.81, f32[1]{0:T(128)} %bitcast.16), channel_id=1, replica_groups=mesh['leaf'=8,'vec'=4] {'vec'}, use_global_device_ids=true, to_apply=%region_14.16 | all-reduce | flops 8193 | bytes 65544 | tf_op jit(solution)/shard_map/psum | solution.py:107
  1489.0 1.7 collective-permute-done.2
  1490.8 25.6 %gather_fusion.6 = f32[4096]{0:T(1024)S(1)} fusion(f32[64,128]{1,0:T(8,128)S(1)} %pad_maximum_fusion.3, s32[4096]{0:T(1024)S(1)} %reshape.488), kind=kCustom, calls=%fused_computation.2.clone | custom fusion | bytes 65536 | tf_op jit(solution)/shard_map/jit(take_along_axis)/gather | solution.py:49
  1517.4 16.0 all-reduce.2
  1536.7 4.4 collective-permute-done.3
  1541.2 25.6 %gather_fusion.7 = f32[4096]{0:T(1024)S(1)} fusion(f32[64,128]{1,0:T(8,128)S(1)} %pad_maximum_fusion.4, s32[4096]{0:T(1024)S(1)} %reshape.494), kind=kCustom, calls=%fused_computation.3.clone | custom fusion | bytes 65536 | tf_op jit(solution)/shard_map/jit(take_along_axis)/gather | solution.py:49
  1567.8 16.5 all-reduce.1
  1587.6 5.3 collective-permute-done.4
  1593.0 25.6 %gather_fusion.8 = f32[4096]{0:T(1024)S(1)} fusion(f32[64,128]{1,0:T(8,128)S(1)} %pad_maximum_fusion.5, s32[4096]{0:T(1024)S(1)} %reshape.500), kind=kCustom, calls=%fused_computation.4.clone | custom fusion | bytes 65536 | tf_op jit(solution)/shard_map/jit(take_along_axis)/gather | solution.py:49
  1619.6 16.1 all-reduce
  1637.7 1.6 collective-permute-start.5
  1639.3 2.5 collective-permute-done.5
  1641.8 4.7 collective-permute-start.6
  1646.6 2.5 collective-permute-done.6
  (338 shorter events, 52.1 us)
Async XLA Ops:
  7.2 836.2 %copy-start = (f32[16,64,64]{2,1,0:T(8,128)S(1)}, f32[16,64,64]{2,1,0:T(8,128)}, u32[]{:S(2)}) copy-start(f32[16,64,64]{2,1,0:T(8,128)} %param.17) | copy-start | bytes 786436
  7.2 18.1 %copy-start.23 = (s32[16,16]{1,0:T(8,128)S(1)}, s32[16,16]{1,0:T(8,128)}, u32[]{:S(2)}) copy-start(s32[16,16]{1,0:T(8,128)} %param.15) | copy-start | bytes 3076
  7.2 836.2 %all-reduce.9.cloned.1.call-start = ((), (), s32[]{:S(2)}) async-start(), calls=%async_computation | async-start | bytes 2097152 | tf_op jit(solution)/shard_map/psum | solution.py:107
  9.4 19.5 %collective-permute-start = (bf16[16,67,256]{2,0,1:T(8,128)(2,1)S(1)}, bf16[16,67,256]{2,0,1:T(8,128)(2,1)}, u32[]{:S(2)}, u32[]{:S(2)}) collective-permute-start(bf16[16,67,256]{2,0,1:T(8,128)(2,1)S(1)} %copy_dynamic-update-slice_fusion), channel_id=1, source_target_pairs={{0,4},{4,8},{8,12},{12,16},{16,20},{20,24},{24,28},{1,5},{5,9},{9,... | collective-permute-start | bytes 1646600 | tf_op jit(solution)/shard_map/ppermute | solution.py:20
  12.6 16.3 collective-permute-start.1
  14.6 9.2 copy-start.7
  15.3 8.5 copy-start.17
  16.0 9.3 copy-start.9
  16.0 9.3 copy-start.11
  16.7 8.6 copy-start.21
  17.4 7.9 copy-start.13
  17.4 7.9 copy-start.15
  18.0 7.2 copy-start.33
  25.2 5.0 copy-start.29
  25.2 5.0 copy-start.31
  25.3 5.0 copy-start.41
  30.3 1.8 copy-start.4
  139.9 644.8 %copy-start.5 = (s32[16,64]{1,0:T(8,128)S(1)}, s32[16,64]{1,0:T(8,128)}, u32[]{:S(2)}) copy-start(s32[16,64]{1,0:T(8,128)} %param.16) | copy-start | bytes 12292
  139.9 644.8 %copy-start.8 = (s32[16,64]{1,0:T(8,128)S(1)}, s32[16,64]{1,0:T(8,128)}, u32[]{:S(2)}) copy-start(s32[16,64]{1,0:T(8,128)} %copy-done.7) | copy-start | bytes 12292
  139.9 644.8 %copy-start.18 = (pred[16,64]{1,0:T(8,128)(4,1)S(1)}, pred[16,64]{1,0:T(8,128)(4,1)}, u32[]{:S(2)}) copy-start(pred[16,64]{1,0:T(8,128)(4,1)} %copy-done.17) | copy-start | bytes 3076
  784.7 2.3 copy-start.27
  784.7 2.9 copy-start.35
  784.7 2.9 copy-start.37
  784.7 2.9 copy-start.39
  784.7 2.9 copy-start.19
  784.7 2.9 copy-start.20
  784.7 2.9 copy-start.43
  786.9 367.1 %all-reduce.11.cloned.1.call-start = ((), (), s32[]{:S(2)}) async-start(), calls=%async_computation.1 | async-start | bytes 524288 | tf_op jit(solution)/shard_map/psum | solution.py:107
  845.7 1.1 copy-start.3
  845.7 1.9 copy-start.1
  847.6 261.9 %copy-start.10 = (s32[8,64]{1,0:T(8,128)S(1)}, s32[8,64]{1,0:T(8,128)}, u32[]{:S(2)}) copy-start(s32[8,64]{1,0:T(8,128)} %copy-done.9) | copy-start | bytes 6148
  847.6 261.9 %copy-start.12 = (s32[8,64]{1,0:T(8,128)S(1)}, s32[8,64]{1,0:T(8,128)}, u32[]{:S(2)}) copy-start(s32[8,64]{1,0:T(8,128)} %copy-done.11) | copy-start | bytes 6148
  847.6 261.9 %copy-start.22 = (pred[8,64]{1,0:T(8,128)(4,1)S(1)}, pred[8,64]{1,0:T(8,128)(4,1)}, u32[]{:S(2)}) copy-start(pred[8,64]{1,0:T(8,128)(4,1)} %copy-done.21) | copy-start | bytes 1540
  1109.4 44.6 %copy-start.45 = (f32[15,64,64]{2,1,0:T(8,128)S(1)}, f32[15,64,64]{2,1,0:T(8,128)}, u32[]{:S(2)}) copy-start(f32[15,64,64]{2,1,0:T(8,128)} %param.19) | copy-start | bytes 737284
  1110.9 45.7 %copy-start.2 = (s32[16384]{0:T(1024)S(1)}, s32[16384]{0:T(1024)}, u32[]{:S(2)}) copy-start(s32[16384]{0:T(1024)} %reshape.441) | copy-start | bytes 196612
  1110.9 220.3 %all-reduce.13.cloned.1.call-start = ((), (), s32[]{:S(2)}) async-start(), calls=%async_computation.2 | async-start | bytes 262144 | tf_op jit(solution)/shard_map/psum | solution.py:107
  1156.6 131.3 %copy-start.14 = (s32[4,64]{1,0:T(4,128)S(1)}, s32[4,64]{1,0:T(4,128)}, u32[]{:S(2)}) copy-start(s32[4,64]{1,0:T(4,128)} %copy-done.13) | copy-start | bytes 3076
  1156.6 131.3 %copy-start.16 = (s32[4,64]{1,0:T(4,128)S(1)}, s32[4,64]{1,0:T(4,128)}, u32[]{:S(2)}) copy-start(s32[4,64]{1,0:T(4,128)} %copy-done.15) | copy-start | bytes 3076
  1156.7 131.3 %copy-start.34 = (pred[4,64]{1,0:T(4,128)(4,1)S(1)}, pred[4,64]{1,0:T(4,128)(4,1)}, u32[]{:S(2)}) copy-start(pred[4,64]{1,0:T(4,128)(4,1)} %copy-done.33) | copy-start | bytes 772
  1289.0 152.6 %all-reduce.15.cloned.1.call-start = ((), (), s32[]{:S(2)}) async-start(), calls=%async_computation.3 | async-start | bytes 131072 | tf_op jit(solution)/shard_map/psum | solution.py:107
  1443.8 25.7 %copy-start.36 = (s32[64]{0:T(128)S(1)}, s32[64]{0:T(128)}, u32[]{:S(2)}) copy-start(s32[64]{0:T(128)} %broadcast_add_fusion.7) | copy-start | bytes 772
  1443.8 25.7 %copy-start.38 = (pred[64]{0:T(512)(128)(4,1)S(1)}, pred[64]{0:T(512)(128)(4,1)}, u32[]{:S(2)}) copy-start(pred[64]{0:T(512)(128)(4,1)} %broadcast_compare_fusion.7) | copy-start | bytes 196
  1443.8 25.7 %copy-start.40 = (s32[64]{0:T(128)S(1)}, s32[64]{0:T(128)}, u32[]{:S(2)}) copy-start(s32[64]{0:T(128)} %slice_bitcast_fusion.4) | copy-start | bytes 772
  1443.8 45.1 %copy-start.26 = (pred[64]{0:T(512)(128)(4,1)S(1)}, pred[64]{0:T(512)(128)(4,1)}, u32[]{:S(2)}) copy-start(pred[64]{0:T(512)(128)(4,1)} %get-tuple-element.218) | copy-start | bytes 196
  1443.8 45.1 %copy-start.28 = (s32[64]{0:T(128)S(1)}, s32[64]{0:T(128)}, u32[]{:S(2)}) copy-start(s32[64]{0:T(128)} %get-tuple-element.219) | copy-start | bytes 772
  1443.8 45.1 %copy-start.44 = (s32[64]{0:T(128)S(1)}, s32[64]{0:T(128)}, u32[]{:S(2)}) copy-start(s32[64]{0:T(128)} %broadcast_add_fusion.5) | copy-start | bytes 772
  1443.8 45.1 %copy-start.6 = (s32[64,64,1]{1,0,2:T(8,128)S(1)}, s32[64,64,1]{1,0,2:T(8,128)}, u32[]{:S(2)}) copy-start(s32[64,64,1]{1,0,2:T(8,128)} %fusion.61) | copy-start | bytes 49156
  1487.6 3.1 collective-permute-start.2
  1490.8 25.7 %copy-start.30 = (pred[64]{0:T(512)(128)(4,1)S(1)}, pred[64]{0:T(512)(128)(4,1)}, u32[]{:S(2)}) copy-start(pred[64]{0:T(512)(128)(4,1)} %copy-done.29) | copy-start | bytes 196
  1490.8 25.7 %copy-start.32 = (s32[64]{0:T(128)S(1)}, s32[64]{0:T(128)}, u32[]{:S(2)}) copy-start(s32[64]{0:T(128)} %copy-done.31) | copy-start | bytes 772
  1490.8 25.7 %copy-start.42 = (s32[64]{0:T(128)S(1)}, s32[64]{0:T(128)}, u32[]{:S(2)}) copy-start(s32[64]{0:T(128)} %copy-done.41) | copy-start | bytes 772
  1490.8 45.8 %copy-start.25 = (s32[64]{0:T(128)S(1)}, s32[64]{0:T(128)}, u32[]{:S(2)}) copy-start(s32[64]{0:T(128)} %get-tuple-element.195) | copy-start | bytes 772
  1535.3 5.8 collective-permute-start.3
  1541.2 46.3 %copy-start.24 = (pred[64]{0:T(512)(128)(4,1)S(1)}, pred[64]{0:T(512)(128)(4,1)}, u32[]{:S(2)}) copy-start(pred[64]{0:T(512)(128)(4,1)} %get-tuple-element.194) | copy-start | bytes 196
  1586.2 6.7 collective-permute-start.4
  1637.7 4.1 collective-permute-start.5
  1641.8 7.2 collective-permute-start.6
  1649.1 2.3 collective-permute-start.7
Sparse Core Ops, SparseCore 0:
  787.0 56.3 all-reduce.8
  1111.0 42.9 all-reduce.10
  1289.1 41.9 all-reduce.12
  1400.2 41.4 all-reduce.14
where the time goes:
time: 1670 us; the launch traced here: 1660 us
  local copies, waits for them, and re-layouts  1250 us (75%)
  waiting for transfers between devices  161 us (10%)
  blocking collectives  103 us (6%)
  matrix products  89.3 us (5%)
  other arithmetic  20.4 us (1%)
  between operations  17.6 us (1%)
    gather x24, local copies, waits for them, and re-layouts, interpolate(): chosen = jnp.take_along_axis(sketch, index_grid, axis=2)  1210 us
    psum x4, waiting for transfers between devices, combine_stats(): return lax.psum((gram_rows, squares), 'vec')  144 us
    psum x8, blocking collectives, combine_stats(): return lax.psum((gram_rows, squares), 'vec')  103 us
    dot_general x16, matrix products, add_slot(): jnp.einsum('nsq,npq->nsp', blocks[:, 3:], kernel_block, preferred_element...  69.9 us
  transfers between devices with their start and end apart: 12, of which 10 were waited for; matrix products, arithmetic and copies ran while one was open for 1% of the time, Pallas kernels for 0%

commit v1 on v0

v1 whole, which is shorter than its diff:
```python
import functools

import jax
import jax.numpy as jnp
from jax import lax
from jax.experimental import pallas as pl
from jax.experimental.pallas import tpu as pltpu
from jax.sharding import PartitionSpec as P

UPL = 3

SOFTEN = 0.0009
EPSILON = 1e-06
VMEM_BYTES = 48 * 1024 * 1024
VMEM = pltpu.MemorySpace.VMEM
SMEM = pltpu.MemorySpace.SMEM


def nt(a, b):
    return lax.dot_general(a, b, (((1,), (1,)), ((), ())), preferred_element_type=jnp.float32)


def nn(a, b):
    return lax.dot_general(a, b, (((1,), (0,)), ((), ())), preferred_element_type=jnp.float32)


def split(a):
    high = a.astype(jnp.bfloat16)
    low = (a - high.astype(jnp.float32)).astype(jnp.bfloat16)
    return high, low


def stacked_split(a):
    high, low = split(a)
    return jnp.concatenate([high, low], axis=0)


def halves(a):
    rows = a.shape[0] // 2
    return a[:rows] + a[rows:]


def near_kernel(tiers, share, count, has_start, halo, own, scaled, refs):
    refs = list(refs)
    nb_ref, points_ref = refs[:2]
    refs = refs[2:]
    probe_ref = refs.pop(0) if own else None
    if halo:
        before_points, after_points, before_probe, after_probe = refs[:4]
        refs = refs[4:]
    start_ref = refs.pop(0) if has_start else None
    outs = [refs.pop(0) for _ in range(len(tiers) if scaled else 1)]
    far, vectors, near, total, tile_a, tile_b, codes = refs

    me = lax.axis_index("vec")
    first = lax.axis_index("leaf") * count
    slots = nb_ref.shape[1]
    rows = len(tiers) * share

    for cluster in range(count):
        far[count + cluster, 0:3, :] = points_ref[cluster].astype(jnp.float32)
    if halo:
        for cluster in range(count):
            far[cluster, 0:3, :] = before_points[cluster].astype(jnp.float32)
            far[2 * count + cluster, 0:3, :] = after_points[cluster].astype(jnp.float32)
        vectors[0:count] = before_probe[...]
        vectors[2 * count : 3 * count] = after_probe[...]
    if own:
        vectors[count : 2 * count] = probe_ref[...]

    codes[0] = rows * 64 + count
    filled = jnp.int32(1)
    for place, tier in enumerate(tiers):
        for part in range(share):
            row = place * share + part
            cluster = (me ^ tier) * share + part

            def add_code(slot, filled, row=row, cluster=cluster):
                listed = nb_ref[cluster, slot]
                position = listed - first + count
                inside = (position >= count) & (position < 2 * count)
                if own and halo:
                    wanted = listed >= 0
                elif own:
                    wanted = (listed >= 0) & inside
                else:
                    wanted = (listed >= 0) & jnp.logical_not(inside)
                codes[filled] = row * 64 + jnp.clip(position, 0, 3 * count - 1)
                return filled + wanted.astype(jnp.int32)

            for slot in range(slots):
                filled = add_code(slot, filled)

    lanes = near.shape[3]
    for place, tier in enumerate(tiers):
        for part in range(share):
            row = place * share + part
            cluster = (me ^ tier) * share + part
            turned = jnp.transpose(far[count + cluster])
            for coordinate in range(3):
                near[row, coordinate] = jnp.broadcast_to(
                    turned[:, coordinate : coordinate + 1], (turned.shape[0], lanes)
                )
    near[rows] = near[0]
    if has_start:
        total[0:rows] = start_ref[...]
        total[rows] = jnp.zeros(total.shape[1:], jnp.float32)
    else:
        total[...] = jnp.zeros(total.shape, jnp.float32)
    tile_b[...] = jnp.zeros(tile_b.shape, tile_b.dtype)
    codes[filled] = rows * 64 + count
    codes[filled + 1] = rows * 64 + count

    size = tile_a.shape[0]

    def multiply(code, tile):
        row = code // 64
        position = code % 64
        total[row] = total[row] + nt(vectors[position], tile[...])

    def evaluate(code, tile):
        row = code // 64
        position = code % 64
        for lane in range(0, size, lanes):
            there = [
                jnp.broadcast_to(
                    far[position, coordinate : coordinate + 1, lane : lane + lanes], (16, lanes)
                )
                for coordinate in range(3)
            ]
            for top in range(0, size, 16):
                distance = SOFTEN
                for coordinate in range(3):
                    gap = near[row, coordinate, top : top + 16, :] - there[coordinate]
                    distance = distance + gap * gap
                tile[top : top + 16, lane : lane + lanes] = lax.rsqrt(distance).astype(
                    jnp.bfloat16
                )

    def step(index, carry):
        code_0 = codes[2 * index]
        code_1 = codes[2 * index + 1]
        code_2 = codes[2 * index + 2]
        multiply(code_0, tile_b)
        evaluate(code_1, tile_a)
        multiply(code_1, tile_a)
        evaluate(code_2, tile_b)
        return carry

    steps = filled // 2
    lax.fori_loop(0, steps, step, 0)
    multiply(codes[2 * steps], tile_b)

    if scaled:
        for place, out in enumerate(outs):
            out[...] = (total[place * share : (place + 1) * share] * 0.015625).astype(out.dtype)
    else:
        outs[0][...] = total[0:rows]


def near_field(tiers, share, nb, points, probe, halo, start, scaled):
    count, columns, size = points.shape[0], (probe if probe is not None else halo[2]).shape[1], points.shape[2]
    rows = len(tiers) * share
    operands = [nb, points]
    if probe is not None:
        operands.append(probe)
    if halo is not None:
        operands.extend(halo)
    if start is not None:
        operands.append(start)
    if scaled:
        outs = [jax.ShapeDtypeStruct((share, columns, size), jnp.bfloat16)] * len(tiers)
    else:
        outs = [jax.ShapeDtypeStruct((rows, columns, size), jnp.float32)]
    body = functools.partial(
        near_kernel, tiers, share, count, start is not None, halo is not None, probe is not None, scaled
    )
    blocks = rows * 6
    return pl.pallas_call(
        lambda *refs: body(refs),
        out_shape=outs,
        in_specs=[pl.BlockSpec(memory_space=SMEM)]
        + [pl.BlockSpec(memory_space=VMEM)] * (len(operands) - 1),
        out_specs=[pl.BlockSpec(memory_space=VMEM)] * len(outs),
        scratch_shapes=[
            pltpu.VMEM((3 * count, 8, size), jnp.float32),
            pltpu.VMEM((3 * count, columns, size), jnp.bfloat16),
            pltpu.VMEM((rows + 1, 3, size, 128), jnp.float32),
            pltpu.VMEM((rows + 1, columns, size), jnp.float32),
            pltpu.VMEM((size, size), jnp.bfloat16),
            pltpu.VMEM((size, size), jnp.bfloat16),
            pltpu.SMEM((rows * nb.shape[1] + 4,), jnp.int32),
        ],
        compiler_params=pltpu.CompilerParams(vmem_limit_bytes=VMEM_BYTES),
        cost_estimate=pl.CostEstimate(
            flops=blocks * size * size * (2 * columns + 10),
            bytes_accessed=8 * rows * columns * size,
            transcendentals=blocks * size * size,
        ),
    )(*operands)


def pivot_factor(pivots, inverse, width):
    chosen = (
        lax.broadcasted_iota(jnp.int32, (width, pivots.shape[1]), 0) == pivots
    ).astype(jnp.bfloat16)
    return nt(stacked_split(jnp.transpose(inverse)), chosen).astype(jnp.bfloat16)


def leaf_node(sketch, pivots, inverse):
    factor = pivot_factor(pivots, inverse, sketch.shape[1])
    wide = sketch.astype(jnp.float32)
    mean_sq = jnp.sum(wide * wide, keepdims=True) / (sketch.shape[0] * sketch.shape[1]) + EPSILON
    scale = 1.0 / (sketch.shape[0] * mean_sq)
    picked = halves(nt(factor, sketch))
    raw = halves(nn(stacked_split(picked), sketch))
    interp = raw * scale
    upward = halves(nt(stacked_split(raw), sketch)) * (scale * lax.rsqrt(mean_sq))
    return interp, upward


def tree_node(sketch, pivots, inverse):
    width, columns = sketch.shape
    factor = pivot_factor(pivots, inverse, width)
    mean_sq = jnp.sum(sketch * sketch, keepdims=True) / (width * columns) + EPSILON
    scale = 1.0 / (columns * mean_sq)
    parts = stacked_split(sketch)
    picked = halves(nn(jnp.concatenate([factor, factor], axis=1), parts))
    raw = halves(nt(stacked_split(picked), parts))
    raw = raw[:, :width] + raw[:, width:]
    interp = raw * scale
    both = stacked_split(raw)
    upward = halves(nn(jnp.concatenate([both, both], axis=1), parts)) * (scale * lax.rsqrt(mean_sq))
    return interp, upward


def device_kernel(
    share,
    group,
    rank,
    own,
    *refs,
):
    parts = group // share
    arrived = refs[: parts - 1]
    pivots, inverse, local_pivots, local_inverse, pack, up_out, sketch, ups = refs[parts - 1 :]
    me = lax.axis_index("vec")
    columns = own.shape[1]
    size = own.shape[2]
    for tier, piece in enumerate((own,) + tuple(arrived)):
        place = pl.ds(pl.multiple_of((me ^ tier) * columns, columns), columns)
        for cluster in range(share):
            sketch[cluster, place, :] = piece[cluster]
    for cluster in range(share):
        row = me * share + cluster
        interp, upward = leaf_node(sketch[cluster], pivots[pl.ds(row, 1), :], inverse[row])
        pack[cluster * rank : (cluster + 1) * rank, :] = interp
        ups[cluster * rank : (cluster + 1) * rank, :] = upward
    level_first, nodes, packed = 0, share // 2, 0
    level_nodes = group // 2
    while nodes >= 1:
        results = []
        for node in range(nodes):
            row = level_first + me * nodes + node
            interp, upward = tree_node(
                ups[2 * node * rank : 2 * (node + 1) * rank, :],
                local_pivots[pl.ds(row, 1), :],
                local_inverse[row],
            )
            top = (share + packed // 2) * rank
            side = (packed % 2) * 2 * rank
            pack[top : top + rank, side : side + 2 * rank] = interp
            results.append(upward)
            packed += 1
        for node, upward in enumerate(results):
            ups[node * rank : (node + 1) * rank, :] = upward
        level_first += level_nodes
        level_nodes //= 2
        nodes //= 2
    up_out[...] = ups[0:rank, :]


def group_kernel(share, group, rank, own, *refs):
    parts = group // share
    arrived = refs[: parts - 1]
    local_pivots, local_inverse, interps, up_out, ups = refs[parts - 1 :]
    me = lax.axis_index("vec")
    for tier, piece in enumerate((own,) + tuple(arrived)):
        ups[pl.ds(pl.multiple_of((me ^ tier) * rank, rank), rank), :] = piece[...]
    row = group - parts
    done = 0
    nodes = parts // 2
    while nodes >= 1:
        results = []
        for node in range(nodes):
            interp, upward = tree_node(
                ups[2 * node * rank : 2 * (node + 1) * rank, :],
                local_pivots[row : row + 1, :],
                local_inverse[row],
            )
            interps[done] = interp
            results.append(upward)
            row += 1
            done += 1
        for node, upward in enumerate(results):
            ups[node * rank : (node + 1) * rank, :] = upward
        nodes //= 2
    up_out[...] = ups[0:rank, :]


def upper_kernel(tier, heap_first, last, rank, own, arrived, pivots, inverse, *refs):
    refs = list(refs)
    if last:
        earlier = [refs.pop(0) for _ in range(tier)]
        interps, top, ups, turned = refs
    else:
        interp_out, up_out, ups = refs
    me = lax.axis_index("leaf")
    side = (me >> tier) & 1
    ups[pl.ds(pl.multiple_of(side * rank, rank), rank), :] = own[...]
    ups[pl.ds(pl.multiple_of((1 - side) * rank, rank), rank), :] = arrived[...]
    node = heap_first + (me >> (tier + 1))
    interp, upward = tree_node(ups[...], pivots[pl.ds(node, 1), :], inverse[node])
    if last:
        for index, ref in enumerate(earlier):
            interps[index] = ref[...]
        interps[tier] = interp
        turned[...] = jnp.transpose(upward)
        columns = top.shape[0]
        place = lax.axis_index("vec") * columns
        top[...] = turned[pl.ds(pl.multiple_of(place, columns), columns), :]
    else:
        interp_out[...] = interp
        up_out[...] = upward


def place_kernel(share, group, rank, own, *refs):
    parts = group // share
    arrived = refs[: parts - 1]
    joined, leaf_out, local_out = refs[parts - 1 :]
    me = lax.axis_index("vec")
    for tier, piece in enumerate((own,) + tuple(arrived)):
        device = me ^ tier
        for cluster in range(share):
            leaf_out[device * share + cluster] = piece[cluster * rank : (cluster + 1) * rank, :]
        level_first, nodes, packed = 0, share // 2, 0
        level_nodes = group // 2
        while nodes >= 1:
            for node in range(nodes):
                top = (share + packed // 2) * rank
                side = (packed % 2) * 2 * rank
                local_out[level_first + device * nodes + node] = piece[
                    top : top + rank, side : side + 2 * rank
                ]
                packed += 1
            level_first += level_nodes
            level_nodes //= 2
            nodes //= 2
    for index in range(parts - 1):
        local_out[group - parts + index] = joined[index]


def call(body, outs, scratch, operands, flops=0):
    return pl.pallas_call(
        body,
        out_shape=outs,
        in_specs=[pl.BlockSpec(memory_space=VMEM)] * len(operands),
        out_specs=jax.tree.map(lambda _: pl.BlockSpec(memory_space=VMEM), outs),
        scratch_shapes=scratch,
        compiler_params=pltpu.CompilerParams(vmem_limit_bytes=VMEM_BYTES),
        cost_estimate=pl.CostEstimate(
            flops=flops, bytes_accessed=sum(o.size * o.dtype.itemsize for o in operands), transcendentals=0
        ),
    )(*operands)


def f32(*shape):
    return jax.ShapeDtypeStruct(shape, jnp.float32)


def on_device(
    points,
    probe_vectors,
    neighbours,
    leaf_pivots,
    leaf_inverse,
    local_pivots,
    local_inverse,
    upper_pivots,
    upper_inverse,
):
    group, columns, size = probe_vectors.shape
    rank = leaf_pivots.shape[1]
    leaf_total = lax.axis_size("leaf")
    parts = lax.axis_size("vec")
    share = group // parts
    total_columns = columns * parts

    up = [(i, i + 1) for i in range(leaf_total - 1)]
    down = [(j, i) for i, j in up]
    halo = (
        lax.ppermute(points, "leaf", up),
        lax.ppermute(points, "leaf", down),
        lax.ppermute(probe_vectors, "leaf", up),
        lax.ppermute(probe_vectors, "leaf", down),
    )

    def vec_send(array, tier):
        return lax.ppermute(array, "vec", [(i, i ^ tier) for i in range(parts)])

    away = list(range(parts - 1, 0, -1))
    started = near_field(away, share, neighbours, points, probe_vectors, None, None, False)[0]
    sent = near_field(away, share, neighbours, points, None, halo, started, True)
    arrived = {tier: vec_send(array, tier) for tier, array in zip(away, sent)}
    kept = near_field([0], share, neighbours, points, probe_vectors, halo, None, True)[0]

    pack_rows = share * rank + (share // 2) * rank
    pack, own_up = call(
        functools.partial(device_kernel, share, group, rank),
        (f32(pack_rows, size), f32(rank, total_columns)),
        [
            pltpu.VMEM((share, total_columns, size), jnp.bfloat16),
            pltpu.VMEM((share * rank, total_columns), jnp.float32),
        ],
        [kept]
        + [arrived[tier] for tier in range(1, parts)]
        + [leaf_pivots, leaf_inverse, local_pivots, local_inverse],
    )
    joined, own_up = call(
        functools.partial(group_kernel, share, group, rank),
        (f32(parts - 1, rank, 2 * rank), f32(rank, total_columns)),
        [pltpu.VMEM((parts * rank, total_columns), jnp.float32)],
        [own_up]
        + [vec_send(own_up, tier) for tier in range(1, parts)]
        + [local_pivots, local_inverse],
    )
    pack, own_up = lax.optimization_barrier((pack, own_up))
    others = [vec_send(pack, tier) for tier in range(1, parts)]

    heap_first = 0
    maps = []
    for tier in range(UPL):
        last = tier == UPL - 1
        partner = lax.ppermute(own_up, "leaf", [(i, i ^ (1 << tier)) for i in range(leaf_total)])
        outs = (f32(rank, 2 * rank), f32(rank, total_columns))
        scratch = [pltpu.VMEM((2 * rank, total_columns), jnp.float32)]
        operands = [own_up, partner, upper_pivots, upper_inverse]
        if last:
            outs = (f32(UPL, rank, 2 * rank), f32(columns, rank))
            scratch.append(pltpu.VMEM((total_columns, rank), jnp.float32))
            operands += maps
        first, own_up = call(
            functools.partial(upper_kernel, tier, heap_first, last, rank), outs, scratch, operands
        )
        maps.append(first)
        heap_first += leaf_total >> (tier + 1)
    leaf_map, local_map = call(
        functools.partial(place_kernel, share, group, rank),
        (f32(group, rank, size), f32(group - 1, rank, 2 * rank)),
        [],
        [pack] + others + [joined],
    )
    return (
        jnp.swapaxes(leaf_map, 1, 2),
        jnp.swapaxes(local_map, 1, 2),
        jnp.swapaxes(first, 1, 2)[None],
        own_up[None],
    )


def solution(mesh):
    placed = (
        P("leaf", None, None),
        P("leaf", "vec", None),
        P("leaf", None),
        P("leaf", None),
        P("leaf", None, None),
        P("leaf", None),
        P("leaf", None, None),
        P(),
        P(),
    )
    return jax.shard_map(
        on_device,
        mesh=mesh,
        in_specs=placed,
        out_specs=(
            P("leaf", None, None),
            P("leaf", None, None),
            P("leaf", None, None, None),
            P("leaf", "vec", None),
        ),
        check_vma=False,
    )
```

time: 1670 us -> 94.9 us (0.06)
  local copies, waits for them, and re-layouts: 1250 us -> 1.83 us
  waiting for transfers between devices: 161 us -> 13 us
  blocking collectives: 103 us -> 0 us
  matrix products: 89.3 us -> 0 us
  Pallas kernels: 0 us -> 49 us
  other arithmetic: 20.4 us -> 0 us
  between operations: 17.6 us -> 0.87 us
    gather x40 -> x0, local copies, waits for them, and re-layouts: 1240 us -> none  [the longest x24 1210 us: interpolate(): chosen = jnp.take_along_axis(sketch, index_grid, axis=2)]
    psum x4 -> x0, waiting for transfers between devices: 144 us -> none  [combine_stats(): return lax.psum((gram_rows, squares), 'vec')]
    psum x8 -> x0, blocking collectives: 103 us -> none  [combine_stats(): return lax.psum((gram_rows, squares), 'vec')]
    dot_general x40 -> x0, matrix products: 89.3 us -> none  [the longest x16 69.9 us: add_slot(): jnp.einsum('nsq,npq->nsp', blocks[:, 3:], kernel_block, preferred_element...]
    pallas_call x0 -> x9, Pallas kernels: none -> 49 us  [the longest x3 41.5 us: near_field(): pl.pallas_call(lambda *refs: body(refs), out_shape=outs, in_specs=[pl.Blo...]
  transfers between devices with their start and end apart: 12 -> 16, of which waited for: 10 -> 6; matrix products, arithmetic and copies ran while one was open for 1% -> 1% of each run, Pallas kernels for 0% -> 33%
where the time goes in v1:
time: 94.9 us; the launch traced here: 93.6 us
  Pallas kernels  49 us (52%)
  starting transfers between devices  29 us (31%)
  waiting for transfers between devices  13 us (14%)
  local copies, waits for them, and re-layouts  1.83 us (2%)
    pallas_call x3, Pallas kernels, near_field(): pl.pallas_call(lambda *refs: body(refs), out_shape=outs, in_specs=[pl.Blo...  41.5 us
    ppermute x9, starting transfers between devices, vec_send(): return lax.ppermute(array, 'vec', [(i, i ^ tier) for i in range(parts)])  10.7 us
    ppermute x3, waiting for transfers between devices, on_device(): lax.ppermute(own_up, 'leaf', [(i, i ^ 1 << tier) for i in range(leaf_tota...  8.13 us
    ppermute x3, starting transfers between devices, on_device(): lax.ppermute(own_up, 'leaf', [(i, i ^ 1 << tier) for i in range(leaf_tota...  8.06 us
    pallas_call x6, Pallas kernels, call(): pl.pallas_call(body, out_shape=outs, in_specs=[pl.BlockSpec(memory_space=...  7.48 us
    ppermute x1, starting transfers between devices, on_device(): lax.ppermute(points, 'leaf', up)  5.19 us
    ppermute x9, waiting for transfers between devices, vec_send(): return lax.ppermute(array, 'vec', [(i, i ^ tier) for i in range(parts)])  4.83 us
    ppermute x1, starting transfers between devices, on_device(): lax.ppermute(probe_vectors, 'leaf', up)  2.39 us
  transfers between devices with their start and end apart: 16, of which 6 were waited for; matrix products, arithmetic and copies ran while one was open for 1% of the time, Pallas kernels for 33%

profile of v1, /device:TPU:0, one launch (start us, length us, event | category | flops | bytes accessed | tf_op | source)
XLA Modules:
  0.0 93.6 jit_solution(15273250006436368461)
XLA Ops:
  0.6 0.0 copy-start.8
  0.6 2.4 %collective-permute-start.2 = (bf16[16,64,256]{2,1,0:T(8,128)(2,1)}, bf16[16,64,256]{2,1,0:T(8,128)(2,1)S(1)}, u32[]{:S(2)}, u32[]{:S(2)}) collective-permute-start(bf16[16,64,256]{2,1,0:T(8,128)(2,1)} %refs_2_.3), channel_id=1, source_target_pairs={{0,4},{4,8},{8,12},{12,16},{16,20},{20,24},{24,28},{1,5},{5,9},{9,... | collective-permute-start | bytes 1572872 | tf_op jit(solution)/shard_map/ppermute | solution.py:404
  3.0 1.3 %collective-permute-start.3 = (bf16[16,64,256]{2,1,0:T(8,128)(2,1)}, bf16[16,64,256]{2,1,0:T(8,128)(2,1)S(1)}, u32[]{:S(2)}, u32[]{:S(2)}) collective-permute-start(bf16[16,64,256]{2,1,0:T(8,128)(2,1)} %refs_2_.3), channel_id=1, source_target_pairs={{4,0},{8,4},{12,8},{16,12},{20,16},{24,20},{28,24},{5,1},{9,5},{13... | collective-permute-start | bytes 1572872 | tf_op jit(solution)/shard_map/ppermute | solution.py:405
  4.3 0.8 copy.15.refs_1_
  5.1 5.2 %collective-permute-start = (bf16[16,3,256]{2,1,0:T(4,128)(2,1)S(1)}, bf16[16,3,256]{2,1,0:T(4,128)(2,1)S(1)}, u32[]{:S(2)}, u32[]{:S(2)}) collective-permute-start(bf16[16,3,256]{2,1,0:T(4,128)(2,1)S(1)} %copy.15.refs_1_), channel_id=1, source_target_pairs={{0,4},{4,8},{8,12},{12,16},{16,20},{20,24},{24,28},{1,5},{5,9},{9,... | collective-permute-start | bytes 73736 | tf_op jit(solution)/shard_map/ppermute | solution.py:402
  10.3 1.3 %collective-permute-start.1 = (bf16[16,3,256]{2,1,0:T(4,128)(2,1)S(1)}, bf16[16,3,256]{2,1,0:T(4,128)(2,1)S(1)}, u32[]{:S(2)}, u32[]{:S(2)}) collective-permute-start(bf16[16,3,256]{2,1,0:T(4,128)(2,1)S(1)} %copy.15.refs_1_), channel_id=1, source_target_pairs={{4,0},{8,4},{12,8},{16,12},{20,16},{24,20},{28,24},{5,1},{9,5},{13... | collective-permute-start | bytes 73736 | tf_op jit(solution)/shard_map/ppermute | solution.py:403
  11.6 0.0 copy-done.8
  11.6 0.0 copy-start.6
  11.6 1.0 %copy-done.6 = bf16[16,64,256]{2,1,0:T(8,128)(2,1)S(1)} copy-done((bf16[16,64,256]{2,1,0:T(8,128)(2,1)S(1)}, bf16[16,64,256]{2,1,0:T(8,128)(2,1)}, u32[]{:S(2)}) %copy-start.6) | copy-done | bytes 524312
  12.7 18.5 %shard_map.121.refs_6_ = f32[12,64,256]{2,1,0:T(8,128)S(1)} custom-call(s32[16,16]{1,0:T(8,128)S(1)} %copy-done.8, bf16[16,3,256]{2,1,0:T(4,128)(2,1)S(1)} %copy.15.refs_1_, bf16[16,64,256]{2,1,0:T(8,128)(2,1)S(1)} %copy-done.6), custom_call_target="tpu_custom_call" | custom-call | flops 651165696 | bytes 1572864 | tf_op jit(solution)/shard_map/pallas_call | solution.py:179
  31.1 0.0 copy-start.7
  31.2 0.0 collective-permute-done.refs_3_.refs_2_
  31.2 0.0 collective-permute-done.1.refs_4_.refs_3_
  31.2 0.0 collective-permute-done.2.refs_5_.refs_4_
  31.2 0.0 collective-permute-done.3.refs_6_.refs_5_
  31.2 13.6 %shard_map.122 = (bf16[4,64,256]{2,1,0:T(8,128)(2,1)S(1)}, bf16[4,64,256]{2,1,0:T(8,128)(2,1)S(1)}, bf16[4,64,256]{2,1,0:T(8,128)(2,1)S(1)}) custom-call(s32[16,16]{1,0:T(8,128)S(1)} %copy-done.8, bf16[16,3,256]{2,1,0:T(4,128)(2,1)S(1)} %copy.15.refs_1_, bf16[16,3,256]{2,1,0:T(4,128)(2,1)S(1)} %collective-permute-done.refs_3_.refs_2_, ...), custom_call_target="tpu_custom_call" | custom-call | flops 651165696 | bytes 1572864 | tf_op jit(solution)/shard_map/pallas_call | solution.py:179
  44.8 1.2 %collective-permute-start.4 = (bf16[4,64,256]{2,1,0:T(8,128)(2,1)S(1)}, bf16[4,64,256]{2,1,0:T(8,128)(2,1)S(1)}, u32[]{:S(2)}, u32[]{:S(2)}) collective-permute-start(bf16[4,64,256]{2,1,0:T(8,128)(2,1)S(1)} %get-tuple-element.21), channel_id=1, source_target_pairs={{0,1},{1,0},{2,3},{3,2},{4,5},{5,4},{6,7},{7,6},{8,9},{9,8},{10,11... | collective-permute-start | bytes 393224 | tf_op jit(solution)/shard_map/ppermute | solution.py:409
  45.9 1.5 %collective-permute-start.5 = (bf16[4,64,256]{2,1,0:T(8,128)(2,1)S(1)}, bf16[4,64,256]{2,1,0:T(8,128)(2,1)S(1)}, u32[]{:S(2)}, u32[]{:S(2)}) collective-permute-start(bf16[4,64,256]{2,1,0:T(8,128)(2,1)S(1)} %get-tuple-element.22), channel_id=1, source_target_pairs={{0,2},{1,3},{2,0},{3,1},{4,6},{5,7},{6,4},{7,5},{8,10},{9,11},{10,... | collective-permute-start | bytes 393224 | tf_op jit(solution)/shard_map/ppermute | solution.py:409
  47.5 0.0 copy-start.1
  47.5 0.0 copy-start.2
  47.5 0.0 copy-start.4
  47.5 0.0 copy-start.5
  47.5 0.9 collective-permute-start.6
  48.4 0.0 copy-done.7
  48.4 9.5 %shard_map.120.own = bf16[4,64,256]{2,1,0:T(8,128)(2,1)S(1)} custom-call(s32[16,16]{1,0:T(8,128)S(1)} %copy-done.8, bf16[16,3,256]{2,1,0:T(4,128)(2,1)S(1)} %copy.15.refs_1_, bf16[16,64,256]{2,1,0:T(8,128)(2,1)S(1)} %copy-done.7, bf16[16,3,256]{2,1,0:T(4,128)(2,1)S(1)} %collective-permute-done.refs_3_.refs_2_, ...), custom_call_target="tpu_custom_call" | custom-call | flops 217055232 | bytes 524288 | tf_op jit(solution)/shard_map/pallas_call | solution.py:179
  57.9 0.0 collective-permute-done.4.refs_0_
  57.9 0.0 collective-permute-done.5.refs_1_
  57.9 0.0 collective-permute-done.6.refs_2_
  57.9 0.0 copy-done.1
  57.9 0.0 copy-done.2
  57.9 0.0 copy-done.4
  57.9 0.0 copy-done.5
  57.9 2.2 %shard_map.123 = (f32[384,256]{1,0:T(8,128)S(1)}, f32[64,256]{1,0:T(8,128)S(1)}) custom-call(bf16[4,64,256]{2,1,0:T(8,128)(2,1)S(1)} %shard_map.120.own, bf16[4,64,256]{2,1,0:T(8,128)(2,1)S(1)} %collective-permute-done.4.refs_0_, bf16[4,64,256]{2,1,0:T(8,128)(2,1)S(1)} %collective-permute-done.5.refs_1_, ...), custom_call_target="tpu_custom_call" | custom-call | bytes 1040128 | tf_op jit(solution)/shard_map/pallas_call | solution.py:364
  60.2 0.0 copy-start
  60.2 1.2 %collective-permute-start.7 = (f32[64,256]{1,0:T(8,128)S(1)}, f32[64,256]{1,0:T(8,128)S(1)}, u32[]{:S(2)}, u32[]{:S(2)}) collective-permute-start(f32[64,256]{1,0:T(8,128)S(1)} %get-tuple-element.25.own), channel_id=1, source_target_pairs={{0,1},{1,0},{2,3},{3,2},{4,5},{5,4},{6,7},{7,6},{8,9},{9,8},{10,11... | collective-permute-start | bytes 196616 | tf_op jit(solution)/shard_map/ppermute | solution.py:409
  61.4 1.9 %collective-permute-start.8 = (f32[64,256]{1,0:T(8,128)S(1)}, f32[64,256]{1,0:T(8,128)S(1)}, u32[]{:S(2)}, u32[]{:S(2)}) collective-permute-start(f32[64,256]{1,0:T(8,128)S(1)} %get-tuple-element.25.own), channel_id=1, source_target_pairs={{0,2},{1,3},{2,0},{3,1},{4,6},{5,7},{6,4},{7,5},{8,10},{9,11},{10,... | collective-permute-start | bytes 196616 | tf_op jit(solution)/shard_map/ppermute | solution.py:409
  63.3 0.5 collective-permute-start.9
  63.7 0.8 collective-permute-done.7.refs_0_
  64.5 1.1 %collective-permute-done.8.refs_1_ = f32[64,256]{1,0:T(8,128)S(1)} collective-permute-done((f32[64,256]{1,0:T(8,128)S(1)}, f32[64,256]{1,0:T(8,128)S(1)}, u32[]{:S(2)}, u32[]{:S(2)}) %collective-permute-start.8) | collective-permute-done | bytes 65568 | tf_op jit(solution)/shard_map/ppermute | solution.py:409
  65.6 2.9 %collective-permute-done.9.refs_2_ = f32[64,256]{1,0:T(8,128)S(1)} collective-permute-done((f32[64,256]{1,0:T(8,128)S(1)}, f32[64,256]{1,0:T(8,128)S(1)}, u32[]{:S(2)}, u32[]{:S(2)}) %collective-permute-start.9) | collective-permute-done | bytes 65568 | tf_op jit(solution)/shard_map/ppermute | solution.py:409
  68.6 0.0 copy-start.3
  68.6 1.5 %shard_map.124 = (f32[3,64,128]{2,1,0:T(8,128)S(1)}, f32[64,256]{1,0:T(8,128)S(1)}) custom-call(f32[64,256]{1,0:T(8,128)S(1)} %get-tuple-element.25.own, f32[64,256]{1,0:T(8,128)S(1)} %collective-permute-done.7.refs_0_, f32[64,256]{1,0:T(8,128)S(1)} %collective-permute-done.8.refs_1_, f32[64,256]{1,0:T(8,128)S(1)} %collective-permute-done.9.refs_2_, ...), custom_call_target="tpu_custom_call" | custom-call | bytes 511744 | tf_op jit(solution)/shard_map/pallas_call | solution.py:364
  70.0 1.2 %collective-permute-start.10 = (f32[384,256]{1,0:T(8,128)S(1)}, f32[384,256]{1,0:T(8,128)S(1)}, u32[]{:S(2)}, u32[]{:S(2)}) collective-permute-start(f32[384,256]{1,0:T(8,128)S(1)} %get-tuple-element.27.own), channel_id=1, source_target_pairs={{0,1},{1,0},{2,3},{3,2},{4,5},{5,4},{6,7},{7,6},{8,9},{9,8},{10,11... | collective-permute-start | bytes 1179656 | tf_op jit(solution)/shard_map/ppermute | solution.py:409
  71.3 0.0 collective-permute-start.11
  71.3 2.3 %collective-permute-start.12 = (f32[384,256]{1,0:T(8,128)S(1)}, f32[384,256]{1,0:T(8,128)S(1)}, u32[]{:S(2)}, u32[]{:S(2)}) collective-permute-start(f32[384,256]{1,0:T(8,128)S(1)} %get-tuple-element.27.own), channel_id=1, source_target_pairs={{0,3},{1,2},{2,1},{3,0},{4,7},{5,6},{6,5},{7,4},{8,11},{9,10},{10,... | collective-permute-start | bytes 1179656 | tf_op jit(solution)/shard_map/ppermute | solution.py:409
  73.6 0.8 collective-permute-start.13
  74.4 0.9 collective-permute-done.13.arrived
  75.3 0.0 copy-done
  75.3 0.0 copy-done.3
  75.3 0.6 shard_map.126
  75.9 6.5 %collective-permute-start.14 = (f32[64,256]{1,0:T(8,128)S(1)}, f32[64,256]{1,0:T(8,128)S(1)}, u32[]{:S(2)}, u32[]{:S(2)}) collective-permute-start(f32[64,256]{1,0:T(8,128)S(1)} %get-tuple-element.32.own), channel_id=1, source_target_pairs={{0,8},{4,12},{8,0},{12,4},{16,24},{20,28},{24,16},{28,20},{1,9},{5... | collective-permute-start | bytes 196616 | tf_op jit(solution)/shard_map/ppermute | solution.py:444
  82.4 2.4 %collective-permute-done.14.arrived = f32[64,256]{1,0:T(8,128)S(1)} collective-permute-done((f32[64,256]{1,0:T(8,128)S(1)}, f32[64,256]{1,0:T(8,128)S(1)}, u32[]{:S(2)}, u32[]{:S(2)}) %collective-permute-start.14) | collective-permute-done | bytes 65568 | tf_op jit(solution)/shard_map/ppermute | solution.py:444
  84.9 0.6 shard_map.127
  85.5 0.7 collective-permute-start.15
  86.2 4.8 %collective-permute-done.15.arrived = f32[64,256]{1,0:T(8,128)S(1)} collective-permute-done((f32[64,256]{1,0:T(8,128)S(1)}, f32[64,256]{1,0:T(8,128)S(1)}, u32[]{:S(2)}, u32[]{:S(2)}) %collective-permute-start.15) | collective-permute-done | bytes 65568 | tf_op jit(solution)/shard_map/ppermute | solution.py:444
  91.0 1.3 %shard_map.128 = (f32[3,64,128]{2,1,0:T(8,128)}, f32[64,64]{1,0:T(8,128)}) custom-call(f32[64,256]{1,0:T(8,128)S(1)} %get-tuple-element.33.own, f32[64,256]{1,0:T(8,128)S(1)} %collective-permute-done.15.arrived, s32[7,64]{1,0:T(8,128)S(1)} %copy-done.3, f32[7,64,64]{2,1,0:T(8,128)S(1)} %copy-done, f32[64,128]{1,0:T(8,128)S(1)} %get-tuple-element.34.refs_0_, ...), custom_call_target="tpu_custom_call" | custom-call | bytes 313088 | tf_op jit(solution)/shard_map/pallas_call | solution.py:364
  92.4 0.0 collective-permute-done.10.refs_0_
  92.4 0.0 collective-permute-done.11.refs_1_
  92.4 0.0 collective-permute-done.12.refs_2_
  92.4 1.2 %shard_map.125 = (f32[16,64,256]{2,1,0:T(8,128)}, f32[15,64,128]{2,1,0:T(8,128)}) custom-call(f32[384,256]{1,0:T(8,128)S(1)} %get-tuple-element.27.own, f32[384,256]{1,0:T(8,128)S(1)} %collective-permute-done.10.refs_0_, f32[384,256]{1,0:T(8,128)S(1)} %collective-permute-done.11.refs_1_, f32[384,256]{1,0:T(8,128)S(1)} %collective-permute-done.12.refs_2_, ...), custom_call_target="tpu_custom_call" | custom-call | bytes 1671168 | tf_op jit(solution)/shard_map/pallas_call | solution.py:364
Async XLA Ops:
  0.6 11.0 %copy-start.8 = (s32[16,16]{1,0:T(8,128)S(1)}, s32[16,16]{1,0:T(8,128)}, u32[]{:S(2)}) copy-start(s32[16,16]{1,0:T(8,128)} %refs_0_.5) | copy-start | bytes 3076
  0.6 30.5 %collective-permute-start.2 = (bf16[16,64,256]{2,1,0:T(8,128)(2,1)}, bf16[16,64,256]{2,1,0:T(8,128)(2,1)S(1)}, u32[]{:S(2)}, u32[]{:S(2)}) collective-permute-start(bf16[16,64,256]{2,1,0:T(8,128)(2,1)} %refs_2_.3), channel_id=1, source_target_pairs={{0,4},{4,8},{8,12},{12,16},{16,20},{20,24},{24,28},{1,5},{5,9},{9,... | collective-permute-start | bytes 1572872 | tf_op jit(solution)/shard_map/ppermute | solution.py:404
  3.0 28.2 %collective-permute-start.3 = (bf16[16,64,256]{2,1,0:T(8,128)(2,1)}, bf16[16,64,256]{2,1,0:T(8,128)(2,1)S(1)}, u32[]{:S(2)}, u32[]{:S(2)}) collective-permute-start(bf16[16,64,256]{2,1,0:T(8,128)(2,1)} %refs_2_.3), channel_id=1, source_target_pairs={{4,0},{8,4},{12,8},{16,12},{20,16},{24,20},{28,24},{5,1},{9,5},{13... | collective-permute-start | bytes 1572872 | tf_op jit(solution)/shard_map/ppermute | solution.py:405
  5.1 26.1 %collective-permute-start = (bf16[16,3,256]{2,1,0:T(4,128)(2,1)S(1)}, bf16[16,3,256]{2,1,0:T(4,128)(2,1)S(1)}, u32[]{:S(2)}, u32[]{:S(2)}) collective-permute-start(bf16[16,3,256]{2,1,0:T(4,128)(2,1)S(1)} %copy.15.refs_1_), channel_id=1, source_target_pairs={{0,4},{4,8},{8,12},{12,16},{16,20},{20,24},{24,28},{1,5},{5,9},{9,... | collective-permute-start | bytes 73736 | tf_op jit(solution)/shard_map/ppermute | solution.py:402
  10.3 20.9 %collective-permute-start.1 = (bf16[16,3,256]{2,1,0:T(4,128)(2,1)S(1)}, bf16[16,3,256]{2,1,0:T(4,128)(2,1)S(1)}, u32[]{:S(2)}, u32[]{:S(2)}) collective-permute-start(bf16[16,3,256]{2,1,0:T(4,128)(2,1)S(1)} %copy.15.refs_1_), channel_id=1, source_target_pairs={{4,0},{8,4},{12,8},{16,12},{20,16},{24,20},{28,24},{5,1},{9,5},{13... | collective-permute-start | bytes 73736 | tf_op jit(solution)/shard_map/ppermute | solution.py:403
  11.6 1.0 %copy-start.6 = (bf16[16,64,256]{2,1,0:T(8,128)(2,1)S(1)}, bf16[16,64,256]{2,1,0:T(8,128)(2,1)}, u32[]{:S(2)}) copy-start(bf16[16,64,256]{2,1,0:T(8,128)(2,1)} %refs_2_.3) | copy-start | bytes 1572868
  31.1 17.3 %copy-start.7 = (bf16[16,64,256]{2,1,0:T(8,128)(2,1)S(1)}, bf16[16,64,256]{2,1,0:T(8,128)(2,1)}, u32[]{:S(2)}) copy-start(bf16[16,64,256]{2,1,0:T(8,128)(2,1)} %refs_2_.3) | copy-start | bytes 1572868
  44.8 13.1 %collective-permute-start.4 = (bf16[4,64,256]{2,1,0:T(8,128)(2,1)S(1)}, bf16[4,64,256]{2,1,0:T(8,128)(2,1)S(1)}, u32[]{:S(2)}, u32[]{:S(2)}) collective-permute-start(bf16[4,64,256]{2,1,0:T(8,128)(2,1)S(1)} %get-tuple-element.21), channel_id=1, source_target_pairs={{0,1},{1,0},{2,3},{3,2},{4,5},{5,4},{6,7},{7,6},{8,9},{9,8},{10,11... | collective-permute-start | bytes 393224 | tf_op jit(solution)/shard_map/ppermute | solution.py:409
  45.9 11.9 %collective-permute-start.5 = (bf16[4,64,256]{2,1,0:T(8,128)(2,1)S(1)}, bf16[4,64,256]{2,1,0:T(8,128)(2,1)S(1)}, u32[]{:S(2)}, u32[]{:S(2)}) collective-permute-start(bf16[4,64,256]{2,1,0:T(8,128)(2,1)S(1)} %get-tuple-element.22), channel_id=1, source_target_pairs={{0,2},{1,3},{2,0},{3,1},{4,6},{5,7},{6,4},{7,5},{8,10},{9,11},{10,... | collective-permute-start | bytes 393224 | tf_op jit(solution)/shard_map/ppermute | solution.py:409
  47.5 10.4 %copy-start.1 = (f32[15,64,64]{2,1,0:T(8,128)S(1)}, f32[15,64,64]{2,1,0:T(8,128)}, u32[]{:S(2)}) copy-start(f32[15,64,64]{2,1,0:T(8,128)} %refs_4_.3) | copy-start | bytes 737284
  47.5 10.4 %copy-start.2 = (f32[16,64,64]{2,1,0:T(8,128)S(1)}, f32[16,64,64]{2,1,0:T(8,128)}, u32[]{:S(2)}) copy-start(f32[16,64,64]{2,1,0:T(8,128)} %refs_4_.2) | copy-start | bytes 786436
  47.5 10.5 %copy-start.4 = (s32[15,64]{1,0:T(8,128)S(1)}, s32[15,64]{1,0:T(8,128)}, u32[]{:S(2)}) copy-start(s32[15,64]{1,0:T(8,128)} %refs_3_.3) | copy-start | bytes 11524
  47.5 10.5 %copy-start.5 = (s32[16,64]{1,0:T(8,128)S(1)}, s32[16,64]{1,0:T(8,128)}, u32[]{:S(2)}) copy-start(s32[16,64]{1,0:T(8,128)} %refs_3_.2) | copy-start | bytes 12292
  47.5 10.4 %collective-permute-start.6 = (bf16[4,64,256]{2,1,0:T(8,128)(2,1)S(1)}, bf16[4,64,256]{2,1,0:T(8,128)(2,1)S(1)}, u32[]{:S(2)}, u32[]{:S(2)}) collective-permute-start(bf16[4,64,256]{2,1,0:T(8,128)(2,1)S(1)} %get-tuple-element.23), channel_id=1, source_target_pairs={{0,3},{1,2},{2,1},{3,0},{4,7},{5,6},{6,5},{7,4},{8,11},{9,10},{10,... | collective-permute-start | bytes 393224 | tf_op jit(solution)/shard_map/ppermute | solution.py:409
  60.2 15.1 %copy-start = (f32[7,64,64]{2,1,0:T(8,128)S(1)}, f32[7,64,64]{2,1,0:T(8,128)}, u32[]{:S(2)}) copy-start(f32[7,64,64]{2,1,0:T(8,128)} %inverse.5) | copy-start | bytes 344068
  60.2 4.3 %collective-permute-start.7 = (f32[64,256]{1,0:T(8,128)S(1)}, f32[64,256]{1,0:T(8,128)S(1)}, u32[]{:S(2)}, u32[]{:S(2)}) collective-permute-start(f32[64,256]{1,0:T(8,128)S(1)} %get-tuple-element.25.own), channel_id=1, source_target_pairs={{0,1},{1,0},{2,3},{3,2},{4,5},{5,4},{6,7},{7,6},{8,9},{9,8},{10,11... | collective-permute-start | bytes 196616 | tf_op jit(solution)/shard_map/ppermute | solution.py:409
  61.4 4.3 %collective-permute-start.8 = (f32[64,256]{1,0:T(8,128)S(1)}, f32[64,256]{1,0:T(8,128)S(1)}, u32[]{:S(2)}, u32[]{:S(2)}) collective-permute-start(f32[64,256]{1,0:T(8,128)S(1)} %get-tuple-element.25.own), channel_id=1, source_target_pairs={{0,2},{1,3},{2,0},{3,1},{4,6},{5,7},{6,4},{7,5},{8,10},{9,11},{10,... | collective-permute-start | bytes 196616 | tf_op jit(solution)/shard_map/ppermute | solution.py:409
  63.3 5.3 %collective-permute-start.9 = (f32[64,256]{1,0:T(8,128)S(1)}, f32[64,256]{1,0:T(8,128)S(1)}, u32[]{:S(2)}, u32[]{:S(2)}) collective-permute-start(f32[64,256]{1,0:T(8,128)S(1)} %get-tuple-element.25.own), channel_id=1, source_target_pairs={{0,3},{1,2},{2,1},{3,0},{4,7},{5,6},{6,5},{7,4},{8,11},{9,10},{10,... | collective-permute-start | bytes 196616 | tf_op jit(solution)/shard_map/ppermute | solution.py:409
  68.6 6.8 %copy-start.3 = (s32[7,64]{1,0:T(8,128)S(1)}, s32[7,64]{1,0:T(8,128)}, u32[]{:S(2)}) copy-start(s32[7,64]{1,0:T(8,128)} %pivots.5) | copy-start | bytes 5380
  70.0 22.3 %collective-permute-start.10 = (f32[384,256]{1,0:T(8,128)S(1)}, f32[384,256]{1,0:T(8,128)S(1)}, u32[]{:S(2)}, u32[]{:S(2)}) collective-permute-start(f32[384,256]{1,0:T(8,128)S(1)} %get-tuple-element.27.own), channel_id=1, source_target_pairs={{0,1},{1,0},{2,3},{3,2},{4,5},{5,4},{6,7},{7,6},{8,9},{9,8},{10,11... | collective-permute-start | bytes 1179656 | tf_op jit(solution)/shard_map/ppermute | solution.py:409
  71.3 21.1 %collective-permute-start.11 = (f32[384,256]{1,0:T(8,128)S(1)}, f32[384,256]{1,0:T(8,128)S(1)}, u32[]{:S(2)}, u32[]{:S(2)}) collective-permute-start(f32[384,256]{1,0:T(8,128)S(1)} %get-tuple-element.27.own), channel_id=1, source_target_pairs={{0,2},{1,3},{2,0},{3,1},{4,6},{5,7},{6,4},{7,5},{8,10},{9,11},{10,... | collective-permute-start | bytes 1179656 | tf_op jit(solution)/shard_map/ppermute | solution.py:409
  71.3 21.1 %collective-permute-start.12 = (f32[384,256]{1,0:T(8,128)S(1)}, f32[384,256]{1,0:T(8,128)S(1)}, u32[]{:S(2)}, u32[]{:S(2)}) collective-permute-start(f32[384,256]{1,0:T(8,128)S(1)} %get-tuple-element.27.own), channel_id=1, source_target_pairs={{0,3},{1,2},{2,1},{3,0},{4,7},{5,6},{6,5},{7,4},{8,11},{9,10},{10,... | collective-permute-start | bytes 1179656 | tf_op jit(solution)/shard_map/ppermute | solution.py:409
  73.6 1.7 %collective-permute-start.13 = (f32[64,256]{1,0:T(8,128)S(1)}, f32[64,256]{1,0:T(8,128)S(1)}, u32[]{:S(2)}, u32[]{:S(2)}) collective-permute-start(f32[64,256]{1,0:T(8,128)S(1)} %get-tuple-element.31.own), channel_id=1, source_target_pairs={{0,4},{4,0},{8,12},{12,8},{16,20},{20,16},{24,28},{28,24},{1,5},{5... | collective-permute-start | bytes 196616 | tf_op jit(solution)/shard_map/ppermute | solution.py:444
  75.9 8.9 %collective-permute-start.14 = (f32[64,256]{1,0:T(8,128)S(1)}, f32[64,256]{1,0:T(8,128)S(1)}, u32[]{:S(2)}, u32[]{:S(2)}) collective-permute-start(f32[64,256]{1,0:T(8,128)S(1)} %get-tuple-element.32.own), channel_id=1, source_target_pairs={{0,8},{4,12},{8,0},{12,4},{16,24},{20,28},{24,16},{28,20},{1,9},{5... | collective-permute-start | bytes 196616 | tf_op jit(solution)/shard_map/ppermute | solution.py:444
  85.5 5.6 %collective-permute-start.15 = (f32[64,256]{1,0:T(8,128)S(1)}, f32[64,256]{1,0:T(8,128)S(1)}, u32[]{:S(2)}, u32[]{:S(2)}) collective-permute-start(f32[64,256]{1,0:T(8,128)S(1)} %get-tuple-element.33.own), channel_id=1, source_target_pairs={{0,16},{4,20},{8,24},{12,28},{16,0},{20,4},{24,8},{28,12},{1,17},{... | collective-permute-start | bytes 196616 | tf_op jit(solution)/shard_map/ppermute | solution.py:444
